TPU v7x, 32 devices: a whole 2x2x4 slice. The times are simulated.
32 devices in a mesh: gx: 4 (over z), gy: 4 (over x, core), gz: 2 (over y).
Axes of the slice: x: 2, y: 2, z: 4, core: 2. Of those that a mesh axis runs over, the one named last changes fastest.
Arguments:
- source: float32 [3, 64, 2048], P(None, 'gx', ('gy', 'gz')), may hold values from -6 to 6
- coef_x: float32 [64, 2048], P('gx', ('gy', 'gz')), may hold values from 0.2 to 5
- coef_y: float32 [64, 2048], P('gx', ('gy', 'gz')), may hold values from 0.2 to 5
- coef_z: float32 [64, 2048], P('gx', ('gy', 'gz')), may hold values from 0.2 to 5
- absorb: float32 [64, 2048], P('gx', ('gy', 'gz')), may hold values from 0.05 to 0.5
Outputs:
- correction: float32 [3, 64, 2048], P(None, 'gx', ('gy', 'gz'))
All inputs are finite; a program needn't handle non-finite values.
Results may differ from a plain program's by a relative error of at most 0.0001.
Values sent between devices are 32-bit elements; how exact they have to be, the bound alone decides.
A program may use at most 64 MiB of HBM per device.

v0:
```python
import jax
import jax.numpy as jnp
from jax import lax
from jax.sharding import PartitionSpec as P

LEVELS = 5
NU = 3
KC = 8


OMEGA = 0.8


def passed_along(array, axis, by):
    peers = lax.axis_size(axis)
    pairs = [(i, i + by) for i in range(peers) if 0 <= i + by < peers]
    return lax.ppermute(array, axis, pairs)


def extended(array, sides, width):
    for axis, dim in sides:
        peers, length = (lax.axis_size(axis), array.shape[dim])
        up = [(i, (i + 1) % peers) for i in range(peers - 1)]
        down = [(j, i) for i, j in up]
        last = lax.slice_in_dim(array, length - width, length, axis=dim)
        first = lax.slice_in_dim(array, 0, width, axis=dim)
        before = lax.ppermute(last, axis, up)
        after = lax.ppermute(first, axis, down)
        array = jnp.concatenate([before, array, after], axis=dim)
    return array


def level_terms(coef_x, coef_y, coef_z, absorb, upper_x, upper_y, upper_z):
    diag = coef_x + upper_x + coef_y + upper_y + coef_z + upper_z + absorb
    return (coef_x, upper_x, coef_y, upper_y, coef_z, upper_z, absorb, diag)


def apply_padded(padded, terms):
    coef_x, upper_x, coef_y, upper_y, coef_z, upper_z, absorb, diag = terms
    centre = padded[..., 1:-1, 1:-1, 1:-1]
    out = coef_x * (centre - padded[..., :-2, 1:-1, 1:-1])
    out = out + upper_x * (centre - padded[..., 2:, 1:-1, 1:-1])
    out = out + coef_y * (centre - padded[..., 1:-1, :-2, 1:-1])
    out = out + upper_y * (centre - padded[..., 1:-1, 2:, 1:-1])
    out = out + coef_z * (centre - padded[..., 1:-1, 1:-1, :-2])
    out = out + upper_z * (centre - padded[..., 1:-1, 1:-1, 2:])
    return out + absorb * centre


def coarsen_coef(coef, keep):
    sizes = coef.shape
    blocks = coef.reshape(sizes[0] // 2, 2, sizes[1] // 2, 2, sizes[2] // 2, 2)
    if keep == 0:
        return blocks[:, 0].sum(axis=(2, 4))
    if keep == 1:
        return blocks[:, :, :, 0].sum(axis=(1, 4))
    return blocks[:, :, :, :, :, 0].sum(axis=(1, 3))


def coarsen_cells(field):
    sizes = field.shape
    lead = sizes[:-3]
    blocks = field.reshape(lead + (sizes[-3] // 2, 2, sizes[-2] // 2, 2, sizes[-1] // 2, 2))
    n = len(lead)
    return blocks.sum(axis=(n + 1, n + 3, n + 5))


def refine_cells(field):
    n = field.ndim
    out = jnp.repeat(field, 2, axis=n - 3)
    out = jnp.repeat(out, 2, axis=n - 2)
    return jnp.repeat(out, 2, axis=n - 1)


def shard_terms(kx, ky, kz, absorb):
    plane_x = passed_along(kx[:1], "gx", -1)
    plane_y = passed_along(ky[:, :1], "gy", -1)
    plane_z = passed_along(kz[:, :, :1], "gz", -1)
    upper_x = jnp.concatenate([kx[1:], plane_x], axis=0)
    upper_y = jnp.concatenate([ky[:, 1:], plane_y], axis=1)
    upper_z = jnp.concatenate([kz[:, :, 1:], plane_z], axis=2)
    return level_terms(kx, ky, kz, absorb, upper_x, upper_y, upper_z)


def padded_shard(field):
    return extended(field, (("gx", 1), ("gy", 2), ("gz", 3)), 1)


def smooth(field, rhs, terms, count, fresh):
    for step in range(count):
        if fresh and step == 0:
            field = OMEGA * rhs / terms[7]
        else:
            field = field + OMEGA * (rhs - apply_padded(padded_shard(field), terms)) / terms[7]
    return field


def body(source, coef_x, coef_y, coef_z, absorb):
    side = coef_x.shape[0]
    batch = source.shape[0]
    source = source.reshape(batch, side, side, side)
    coef_x = coef_x.reshape(side, side, side)
    coef_y = coef_y.reshape(side, side, side)
    coef_z = coef_z.reshape(side, side, side)
    absorb = absorb.reshape(side, side, side)
    shapes = []
    kx, ky, kz, sa = (coef_x, coef_y, coef_z, absorb)
    for level in range(LEVELS):
        shapes.append((kx, ky, kz, sa))
        if level + 1 < LEVELS:
            kx, ky, kz, sa = (
                coarsen_coef(kx, 0),
                coarsen_coef(ky, 1),
                coarsen_coef(kz, 2),
                coarsen_cells(sa),
            )
    start = LEVELS - 1
    levels = [shard_terms(*shapes[level]) for level in range(start)]
    rhs = source
    kept = []
    for level in range(start):
        terms = levels[level]
        field = smooth(rhs, rhs, terms, NU, True)
        kept.append((field, rhs))
        rhs = coarsen_cells(rhs - apply_padded(padded_shard(field), terms))
    coarse_terms = shard_terms(*shapes[LEVELS - 1])
    field = smooth(rhs, rhs, coarse_terms, KC, True)
    for level in range(start - 1, -1, -1):
        own, rhs = kept[level]
        field = own + refine_cells(field)
        field = smooth(field, rhs, levels[level], NU, False)
    return field.reshape(batch, side, side * side)


def solution(mesh):
    placed = (
        P(None, "gx", ("gy", "gz")),
        P("gx", ("gy", "gz")),
        P("gx", ("gy", "gz")),
        P("gx", ("gy", "gz")),
        P("gx", ("gy", "gz")),
    )
    return jax.shard_map(
        body, mesh=mesh, in_specs=placed, out_specs=P(None, "gx", ("gy", "gz")), check_vma=False
    )
```

profile of v0, /device:TPU:0, one launch (start us, length us, event | category | flops | bytes accessed | tf_op | source)
XLA Modules:
  0.0 813.3 jit_solution(7922893248284312592)
XLA Ops:
  29.6 4.5 collective-permute-start.7
  44.7 4.5 collective-permute-start.9
  130.5 4.4 collective-permute-done.29
  150.2 6.1 collective-permute-done.33
  162.5 4.7 collective-permute-done.35
  187.9 4.5 collective-permute-done.40
  192.4 4.6 collective-permute-done.41
  232.3 5.3 collective-permute-done.54
  262.5 5.1 collective-permute-start.61
  287.1 6.0 collective-permute-done.69
  365.5 4.4 divide_add_fusion.16
  391.3 4.4 divide_add_fusion.15
  396.9 4.5 collective-permute-start.99
  416.8 4.4 divide_add_fusion.14
  444.8 4.4 divide_add_fusion.13
  470.7 4.4 divide_add_fusion.12
  496.5 4.4 divide_add_fusion.11
  522.2 4.4 fusion.556
  681.1 4.7 collective-permute-done.170
  705.5 4.9 collective-permute-done.176
  730.2 4.7 collective-permute-done.182
  739.2 4.4 collective-permute-done.184
  764.0 4.5 collective-permute-done.190
  789.4 4.4 collective-permute-done.196
  (739 shorter events, 692.4 us)
Async XLA Ops:
  0.8 10.8 %collective-permute-start.2 = (f32[16,16,1]{2,1,0:T(8,128)S(1)}, f32[16,16,1]{2,1,0:T(8,128)S(1)}, u32[]{:S(2)}, u32[]{:S(2)}) collective-permute-start(f32[16,16,1]{2,1,0:T(8,128)S(1)} %bitcast.75), channel_id=1, source_target_pairs={{1,0},{3,2},{5,4},{7,6},{9,8},{11,10},{13,12},{15,14},{17,16},{19,... | collective-permute-start | bytes 3080 | tf_op jit(solution)/shard_map/ppermute | solution.py:17
  3.0 8.7 %collective-permute-start.1 = (f32[16,1,16]{2,1,0:T(1,128)S(1)}, f32[16,1,16]{2,1,0:T(1,128)S(1)}, u32[]{:S(2)}, u32[]{:S(2)}) collective-permute-start(f32[16,1,16]{2,1,0:T(1,128)S(1)} %slice.1558), channel_id=1, source_target_pairs={{2,0},{4,2},{6,4},{3,1},{5,3},{7,5},{10,8},{12,10},{14,12},{11,9},... | collective-permute-start | bytes 3080 | tf_op jit(solution)/shard_map/ppermute | solution.py:17
  60.8 8.0 collective-permute-start.13
  65.4 31.4 %collective-permute-start.23 = (f32[8,8,1]{2,1,0:T(8,128)S(1)}, f32[8,8,1]{2,1,0:T(8,128)S(1)}, u32[]{:S(2)}, u32[]{:S(2)}) collective-permute-start(f32[8,8,1]{2,1,0:T(8,128)S(1)} %bitcast.76), channel_id=1, source_target_pairs={{1,0},{3,2},{5,4},{7,6},{9,8},{11,10},{13,12},{15,14},{17,16},{19,... | collective-permute-start | bytes 776 | tf_op jit(solution)/shard_map/ppermute | solution.py:17
  72.8 8.0 collective-permute-start.15
  78.5 18.2 %collective-permute-start.21 = (f32[1,8,8]{2,1,0:T(8,128)S(1)}, f32[1,8,8]{2,1,0:T(8,128)S(1)}, u32[]{:S(2)}, u32[]{:S(2)}) collective-permute-start(f32[1,8,8]{2,1,0:T(8,128)S(1)} %slice.1575), channel_id=1, source_target_pairs={{8,0},{16,8},{24,16},{9,1},{17,9},{25,17},{10,2},{18,10},{26,18},{... | collective-permute-start | bytes 776 | tf_op jit(solution)/shard_map/ppermute | solution.py:17
  86.7 10.1 %collective-permute-start.22 = (f32[8,1,8]{2,1,0:T(1,128)S(1)}, f32[8,1,8]{2,1,0:T(1,128)S(1)}, u32[]{:S(2)}, u32[]{:S(2)}) collective-permute-start(f32[8,1,8]{2,1,0:T(1,128)S(1)} %slice.1578), channel_id=1, source_target_pairs={{2,0},{4,2},{6,4},{3,1},{5,3},{7,5},{10,8},{12,10},{14,12},{11,9},... | collective-permute-start | bytes 776 | tf_op jit(solution)/shard_map/ppermute | solution.py:17
  119.7 66.8 %collective-permute-start.44 = (f32[4,4,1]{2,1,0:T(4,128)S(1)}, f32[4,4,1]{2,1,0:T(4,128)S(1)}, u32[]{:S(2)}, u32[]{:S(2)}) collective-permute-start(f32[4,4,1]{2,1,0:T(4,128)S(1)} %bitcast.78), channel_id=1, source_target_pairs={{1,0},{3,2},{5,4},{7,6},{9,8},{11,10},{13,12},{15,14},{17,16},{19,... | collective-permute-start | bytes 200 | tf_op jit(solution)/shard_map/ppermute | solution.py:17
  126.8 8.1 collective-permute-start.29
  128.2 59.6 %collective-permute-start.42 = (f32[1,4,4]{2,1,0:T(4,128)S(1)}, f32[1,4,4]{2,1,0:T(4,128)S(1)}, u32[]{:S(2)}, u32[]{:S(2)}) collective-permute-start(f32[1,4,4]{2,1,0:T(4,128)S(1)} %slice.1596), channel_id=1, source_target_pairs={{8,0},{16,8},{24,16},{9,1},{17,9},{25,17},{10,2},{18,10},{26,18},{... | collective-permute-start | bytes 200 | tf_op jit(solution)/shard_map/ppermute | solution.py:17
  141.2 46.6 %collective-permute-start.43 = (f32[4,1,4]{2,1,0:T(1,128)S(1)}, f32[4,1,4]{2,1,0:T(1,128)S(1)}, u32[]{:S(2)}, u32[]{:S(2)}) collective-permute-start(f32[4,1,4]{2,1,0:T(1,128)S(1)} %slice.1599), channel_id=1, source_target_pairs={{2,0},{4,2},{6,4},{3,1},{5,3},{7,5},{10,8},{12,10},{14,12},{11,9},... | collective-permute-start | bytes 200 | tf_op jit(solution)/shard_map/ppermute | solution.py:17
  148.8 7.5 collective-permute-start.33
  157.9 9.3 %collective-permute-start.35 = (f32[3,10,10,1]{3,2,1,0:T(8,128)S(1)}, f32[3,10,10,1]{3,2,1,0:T(8,128)S(1)}, u32[]{:S(2)}, u32[]{:S(2)}) collective-permute-start(f32[3,10,10,1]{3,2,1,0:T(8,128)S(1)} %get-tuple-element.61), channel_id=1, source_target_pairs={{1,0},{3,2},{5,4},{7,6},{9,8},{11,10},{13,12},{15,14},{17,16},{19,... | collective-permute-start | bytes 3608 | tf_op jit(solution)/shard_map/ppermute | solution.py:28
  180.4 82.1 %collective-permute-start.65 = (f32[2,2,1]{2,1,0:T(2,128)S(1)}, f32[2,2,1]{2,1,0:T(2,128)S(1)}, u32[]{:S(2)}, u32[]{:S(2)}) collective-permute-start(f32[2,2,1]{2,1,0:T(2,128)S(1)} %get-tuple-element.165), channel_id=1, source_target_pairs={{1,0},{3,2},{5,4},{7,6},{9,8},{11,10},{13,12},{15,14},{17,16},{19,... | collective-permute-start | bytes 56 | tf_op jit(solution)/shard_map/ppermute | solution.py:17
  182.6 9.8 %collective-permute-start.40 = (f32[3,10,10,1]{3,2,1,0:T(8,128)S(1)}, f32[3,10,10,1]{3,2,1,0:T(8,128)S(1)}, u32[]{:S(2)}, u32[]{:S(2)}) collective-permute-start(f32[3,10,10,1]{3,2,1,0:T(8,128)S(1)} %get-tuple-element.58), channel_id=1, source_target_pairs={{0,1},{2,3},{4,5},{6,7},{8,9},{10,11},{12,13},{14,15},{16,17},{18,... | collective-permute-start | bytes 3608 | tf_op jit(solution)/shard_map/ppermute | solution.py:27
  186.5 10.5 %collective-permute-start.41 = (f32[3,10,10,1]{3,2,1,0:T(8,128)S(1)}, f32[3,10,10,1]{3,2,1,0:T(8,128)S(1)}, u32[]{:S(2)}, u32[]{:S(2)}) collective-permute-start(f32[3,10,10,1]{3,2,1,0:T(8,128)S(1)} %get-tuple-element.59), channel_id=1, source_target_pairs={{1,0},{3,2},{5,4},{7,6},{9,8},{11,10},{13,12},{15,14},{17,16},{19,... | collective-permute-start | bytes 3608 | tf_op jit(solution)/shard_map/ppermute | solution.py:28
  201.4 66.2 %collective-permute-start.63 = (f32[1,2,2]{2,1,0:T(2,128)S(1)}, f32[1,2,2]{2,1,0:T(2,128)S(1)}, u32[]{:S(2)}, u32[]{:S(2)}) collective-permute-start(f32[1,2,2]{2,1,0:T(2,128)S(1)} %get-tuple-element.167), channel_id=1, source_target_pairs={{8,0},{16,8},{24,16},{9,1},{17,9},{25,17},{10,2},{18,10},{26,18},{... | collective-permute-start | bytes 56 | tf_op jit(solution)/shard_map/ppermute | solution.py:17
  208.8 47.4 %collective-permute-start.84 = (f32[1,1,1]{2,1,0:T(1,128)}, f32[1,1,1]{2,1,0:T(1,128)}, u32[]{:S(2)}, u32[]{:S(2)}) collective-permute-start(f32[1,1,1]{2,1,0:T(1,128)} %bitcast.3), channel_id=1, source_target_pairs={{8,0},{16,8},{24,16},{9,1},{17,9},{25,17},{10,2},{18,10},{26,18},{... | collective-permute-start | bytes 20 | tf_op jit(solution)/shard_map/ppermute | solution.py:17
  249.9 46.2 %collective-permute-start.85 = (f32[1,1,1]{2,1,0:T(1,128)}, f32[1,1,1]{2,1,0:T(1,128)}, u32[]{:S(2)}, u32[]{:S(2)}) collective-permute-start(f32[1,1,1]{2,1,0:T(1,128)} %bitcast.5), channel_id=1, source_target_pairs={{2,0},{4,2},{6,4},{3,1},{5,3},{7,5},{10,8},{12,10},{14,12},{11,9},... | collective-permute-start | bytes 20 | tf_op jit(solution)/shard_map/ppermute | solution.py:17
  259.4 9.6 %collective-permute-start.64 = (f32[2,1,2]{2,1,0:T(1,128)S(1)}, f32[2,1,2]{2,1,0:T(1,128)S(1)}, u32[]{:S(2)}, u32[]{:S(2)}) collective-permute-start(f32[2,1,2]{2,1,0:T(1,128)S(1)} %get-tuple-element.169), channel_id=1, source_target_pairs={{2,0},{4,2},{6,4},{3,1},{5,3},{7,5},{10,8},{12,10},{14,12},{11,9},... | collective-permute-start | bytes 56 | tf_op jit(solution)/shard_map/ppermute | solution.py:17
  261.1 57.0 %collective-permute-start.86 = (f32[1,1,1]{2,1,0:T(1,128)}, f32[1,1,1]{2,1,0:T(1,128)}, u32[]{:S(2)}, u32[]{:S(2)}) collective-permute-start(f32[1,1,1]{2,1,0:T(1,128)} %bitcast.7), channel_id=1, source_target_pairs={{1,0},{3,2},{5,4},{7,6},{9,8},{11,10},{13,12},{15,14},{17,16},{19,... | collective-permute-start | bytes 20 | tf_op jit(solution)/shard_map/ppermute | solution.py:17
  676.3 9.5 %collective-permute-start.170 = (f32[3,10,10,1]{3,2,1,0:T(8,128)S(1)}, f32[3,10,10,1]{3,2,1,0:T(8,128)S(1)}, u32[]{:S(2)}, u32[]{:S(2)}) collective-permute-start(f32[3,10,10,1]{3,2,1,0:T(8,128)S(1)} %get-tuple-element.57), channel_id=1, source_target_pairs={{1,0},{3,2},{5,4},{7,6},{9,8},{11,10},{13,12},{15,14},{17,16},{19,... | collective-permute-start | bytes 3608 | tf_op jit(solution)/shard_map/ppermute | solution.py:28
  700.9 9.5 %collective-permute-start.176 = (f32[3,10,10,1]{3,2,1,0:T(8,128)S(1)}, f32[3,10,10,1]{3,2,1,0:T(8,128)S(1)}, u32[]{:S(2)}, u32[]{:S(2)}) collective-permute-start(f32[3,10,10,1]{3,2,1,0:T(8,128)S(1)} %get-tuple-element.55), channel_id=1, source_target_pairs={{1,0},{3,2},{5,4},{7,6},{9,8},{11,10},{13,12},{15,14},{17,16},{19,... | collective-permute-start | bytes 3608 | tf_op jit(solution)/shard_map/ppermute | solution.py:28
  725.5 9.3 %collective-permute-start.182 = (f32[3,10,10,1]{3,2,1,0:T(8,128)S(1)}, f32[3,10,10,1]{3,2,1,0:T(8,128)S(1)}, u32[]{:S(2)}, u32[]{:S(2)}) collective-permute-start(f32[3,10,10,1]{3,2,1,0:T(8,128)S(1)} %get-tuple-element.53), channel_id=1, source_target_pairs={{1,0},{3,2},{5,4},{7,6},{9,8},{11,10},{13,12},{15,14},{17,16},{19,... | collective-permute-start | bytes 3608 | tf_op jit(solution)/shard_map/ppermute | solution.py:28
  (225 other events, 2497.1 us)
where the time goes:
time: 828 us; the launch traced here: 813 us
  waiting for transfers between devices  378 us (46%)
  starting transfers between devices  336 us (41%)
  other arithmetic  53.5 us (6%)
  local copies, waits for them, and re-layouts  38.3 us (5%)
  between operations  8.38 us (1%)
    ppermute x93, waiting for transfers between devices, extended(): after = lax.ppermute(first, axis, down)  351 us
    ppermute x93, starting transfers between devices, extended(): before = lax.ppermute(last, axis, up)  195 us
    ppermute x93, starting transfers between devices, extended(): after = lax.ppermute(first, axis, down)  121 us
    add x27, other arithmetic, smooth(): field + OMEGA * (rhs - apply_padded(padded_shard(field), terms)) / terms[7]  42.4 us
    ppermute x93, waiting for transfers between devices, extended(): before = lax.ppermute(last, axis, up)  25.2 us
    ppermute x15, starting transfers between devices, passed_along(): return lax.ppermute(array, axis, pairs)  19.5 us
  transfers between devices with their start and end apart: 201, of which 112 were waited for; matrix products, arithmetic and copies ran while one was open for 4% of the time, Pallas kernels for 0%

commit v1 on v0

--- a/solution.py
+++ b/solution.py
@@ -1,6 +1,10 @@
+import functools
+
 import jax
 import jax.numpy as jnp
 from jax import lax
+from jax.experimental import pallas as pl
+from jax.experimental.pallas import tpu as pltpu
 from jax.sharding import PartitionSpec as P
 
 LEVELS = 5
@@ -132,6 +136,446 @@
     return field.reshape(batch, side, side * side)
 
 
+MESH_AXES = ("gx", "gy", "gz")
+GATHER_CELLS = 32768
+F32 = jnp.float32
+BF16 = jnp.bfloat16
+
+
+def iota2(shape, dim):
+    return lax.broadcasted_iota(jnp.int32, shape, dim)
+
+
+def split_dot(values, selector, transposed=False):
+    dims = (((1,), (1,)), ((), ())) if transposed else (((1,), (0,)), ((), ()))
+    high = values.astype(BF16)
+    rest = values - high.astype(F32)
+    mid = rest.astype(BF16)
+    low = (rest - mid.astype(F32)).astype(BF16)
+
+    def one(part):
+        return lax.dot_general(part, selector, dims, preferred_element_type=F32)
+
+    return one(high) + (one(mid) + one(low))
+
+
+def selector(lanes, nz, cells, coarse_nz, offset):
+    fine = iota2((lanes, 128), 0)
+    coarse = iota2((lanes, 128), 1)
+    target = (fine // nz // 2) * coarse_nz + (fine % nz) // 2 + offset
+    hit = jnp.where((target == coarse) & (fine < cells), 1.0, 0.0)
+    return hit.astype(BF16)
+
+
+def paired_rows(tmp, rows):
+    return tmp[pl.ds(0, rows, stride=2), :], tmp[pl.ds(1, rows, stride=2), :]
+
+
+def doubled_rows(tmp, values):
+    rows = values.shape[0]
+    tmp[pl.ds(0, rows, stride=2), :] = values
+    tmp[pl.ds(1, rows, stride=2), :] = values
+    return tmp[0 : 2 * rows, :]
+
+
+def roll(values, by, axis):
+    return pltpu.roll(values, by % values.shape[axis], axis)
+
+
+def stencil(field, terms, nz):
+    lanes = field.shape[1]
+    rows = field.shape[0]
+    out = terms[0] * pltpu.roll(field, 1, 0) + terms[1] * pltpu.roll(field, rows - 1, 0)
+    out = out + (terms[2] * pltpu.roll(field, nz, 1) + terms[3] * pltpu.roll(field, lanes - nz, 1))
+    return out + (terms[4] * pltpu.roll(field, 1, 1) + terms[5] * pltpu.roll(field, lanes - 1, 1))
+
+
+def coarse_coefs(stack, sel, tmp, ny_even, nz_even):
+    kx, ky, kz, sa = stack
+    rows = kx.shape[0]
+    joined = jnp.concatenate([kx, jnp.where(ny_even, ky, 0.0), jnp.where(nz_even, kz, 0.0), sa], axis=0)
+    tmp[0 : 4 * rows, :] = split_dot(joined, sel)
+    even, odd = paired_rows(tmp, 2 * rows)
+    half = rows // 2
+    first = even[:half]
+    rest = even[half:] + odd[half:]
+    return first, rest[:half], rest[half : 2 * half], rest[2 * half :]
+
+
+def whole_terms(stack, nx, ny, nz):
+    kx, ky, kz, sa = stack
+    rows, lanes = kx.shape
+    x = iota2((rows, lanes), 0)
+    lane = iota2((rows, lanes), 1)
+    y, z = lane // nz, lane % nz
+    real = (x < nx) & (y < ny)
+    up_x = jnp.where(x < nx - 1, pltpu.roll(kx, rows - 1, 0), 0.0)
+    up_y = jnp.where(y < ny - 1, roll(ky, -nz, 1), 0.0)
+    up_z = jnp.where(z < nz - 1, roll(kz, -1, 1), 0.0)
+    diag = kx + up_x + ky + up_y + kz + up_z + sa
+    weight = jnp.where(real, OMEGA / jnp.where(real, diag, 1.0), 0.0)
+    zero = jnp.zeros_like(kx)
+    return (
+        jnp.where(x > 0, kx * weight, 0.0),
+        jnp.where(real, up_x * weight, 0.0),
+        jnp.where(y > 0, ky * weight, 0.0),
+        jnp.where(real, up_y * weight, 0.0),
+        jnp.where(z > 0, kz * weight, 0.0),
+        jnp.where(real, up_z * weight, 0.0),
+        weight,
+        jnp.where(real, diag * (1.0 / OMEGA), zero),
+    )
+
+
+def cycle_kernel(peers, side, batch, src, kx_ref, ky_ref, kz_ref, sa_ref, out, u_s, xs, xr, yr, zs, zr,
+                 cxr, cyr, czr, tmp, tile, zpart, full, kterms, t1, t2, t3, t4, ctile, czpart, cfull, back,
+                 hsend, hrecv, gsend, grecv):
+    gxn, gyn, gzn = peers
+    gx, gy, gz = lax.axis_index("gx"), lax.axis_index("gy"), lax.axis_index("gz")
+    lanes = side * side
+    last = lanes - 128
+    MESH = pl.DeviceIdType.MESH
+
+    def at_x(i):
+        return (i, gy, gz)
+
+    def at_y(i):
+        return (gx, i, gz)
+
+    partner = (gx, gy, 1 - gz)
+    others = [at_x(lax.rem(gx + d, gxn)) for d in range(1, gxn)]
+    others += [at_y(lax.rem(gy + d, gyn)) for d in range(1, gyn)]
+    others += [partner]
+
+    xs[...] = jnp.zeros_like(xs)
+    xr[...] = jnp.zeros_like(xr)
+    yr[...] = jnp.zeros_like(yr)
+    cxr[...] = jnp.zeros_like(cxr)
+    cyr[...] = jnp.zeros_like(cyr)
+
+    barrier = pltpu.get_barrier_semaphore()
+    for peer in others:
+        pl.semaphore_signal(barrier, inc=1, device_id=peer, device_id_type=MESH)
+    pl.semaphore_wait(barrier, len(others))
+
+    pending = []
+
+    def copy(a, b, s, r, peer):
+        return pltpu.make_async_remote_copy(
+            src_ref=a, dst_ref=b, send_sem=s, recv_sem=r, device_id=peer, device_id_type=MESH
+        )
+
+    def start(c, when=None):
+        if when is None:
+            c.start()
+        else:
+            pl.when(when)(c.start)
+
+    def wait(c, kind, when=None):
+        run = c.wait_recv if kind == "recv" else c.wait_send
+        if when is None:
+            run()
+        else:
+            pl.when(when)(run)
+
+    has_lo_x, has_hi_x = gx > 0, gx < gxn - 1
+    has_lo_y, has_hi_y = gy > 0, gy < gyn - 1
+
+    nk = NU * 2
+    c_x = copy(kx_ref.at[0:8], cxr, hsend.at[nk, 0], hrecv.at[nk, 0], at_x(gx - 1))
+    c_y = copy(ky_ref.at[:, 0:128], cyr, hsend.at[nk, 1], hrecv.at[nk, 1], at_y(gy - 1))
+    c_z = copy(kz_ref, czr, hsend.at[nk, 2], hrecv.at[nk, 2], partner)
+    start(c_x, has_lo_x)
+    start(c_y, has_lo_y)
+    start(c_z)
+    pending += [(c_x, has_lo_x), (c_y, has_lo_y), (c_z, None)]
+
+    kx, ky, kz, sa = kx_ref[...], ky_ref[...], kz_ref[...], sa_ref[...]
+    x = iota2((side, lanes), 0)
+    lane = iota2((side, lanes), 1)
+    y, z = lane // side, lane % side
+    half = side // 2
+    nz1 = half * gzn
+    sel0 = selector(lanes, side, lanes, nz1, gz * half)
+    even_y, even_z = (y % 2) == 0, (z % 2) == 0
+    coarse = coarse_coefs((kx, ky, kz, sa), sel0, tmp, even_y, even_z)
+    for i in range(4):
+        ctile[i] = coarse[i]
+
+    mine_x, mine_y = pl.ds(pl.multiple_of(gx * half, half), half), pl.ds(pl.multiple_of(gy * 128, 128), 128)
+
+    def gather_z(a, b, base):
+        c = copy(a, b, gsend.at[base], grecv.at[base], partner)
+        start(c)
+        pending.append((c, None))
+        return [c]
+
+    def gather_x(whole, base):
+        cs = []
+        for d in range(1, gxn):
+            ref = whole.at[:, mine_x, mine_y]
+            cs.append(copy(ref, ref, gsend.at[base + d], grecv.at[base + d], at_x(lax.rem(gx + d, gxn))))
+        for c in cs:
+            start(c)
+            pending.append((c, None))
+        return cs
+
+    def gather_y(whole, base):
+        cs = []
+        for d in range(1, gyn):
+            ref = whole.at[:, :, mine_y]
+            cs.append(
+                copy(ref, ref, gsend.at[base + gxn + d], grecv.at[base + gxn + d], at_y(lax.rem(gy + d, gyn)))
+            )
+        for c in cs:
+            start(c)
+            pending.append((c, None))
+        return cs
+
+    def landed(cs):
+        for c in cs:
+            wait(c, "recv")
+
+    cbase = gxn + gyn
+    g = gather_z(ctile, czpart, cbase)
+
+    wait(c_x, "recv", has_hi_x)
+    wait(c_y, "recv", has_hi_y)
+    wait(c_z, "recv")
+
+    ylo_mask = (iota2((side, 128), 1) < side)
+    yhi_mask = (iota2((side, 128), 1) >= 128 - side)
+    first_z, last_z = z == 0, z == side - 1
+    up_x = jnp.where(x == side - 1, jnp.broadcast_to(cxr[0:1, :], (side, lanes)), roll(kx, -1, 0))
+    from_y = jnp.where(yhi_mask, roll(cyr[...], -side, 1), 0.0)
+    up_y = roll(ky, -side, 1)
+    up_y = jnp.where(y == side - 1, 0.0, up_y)
+    tail = up_y[:, last:] + from_y
+    up_y = tail if last == 0 else jnp.concatenate([up_y[:, :last], tail], axis=1)
+    low_z = gz == 0
+    from_z = jnp.where(low_z, roll(czr[...], side - 1, 1), 0.0)
+    up_z = jnp.where(last_z, from_z, roll(kz, -1, 1))
+    diag = kx + up_x + ky + up_y + kz + up_z + sa
+    weight = OMEGA / diag
+    wx, wux, wy, wuy, wz, wuz = [k * weight for k in (kx, up_x, ky, up_y, kz, up_z)]
+    inner = (
+        jnp.where(x > 0, wx, 0.0),
+        jnp.where(x < side - 1, wux, 0.0),
+        jnp.where(y > 0, wy, 0.0),
+        jnp.where(y < side - 1, wuy, 0.0),
+        jnp.where(first_z, 0.0, wz),
+        jnp.where(last_z, 0.0, wuz),
+    )
+    for i in range(6):
+        kterms[i] = inner[i]
+    kterms[6] = weight
+    kterms[7] = diag * (1.0 / OMEGA)
+    kterms[8] = jnp.where((x == 0) & has_lo_x, wx, 0.0)
+    kterms[9] = jnp.where(x == side - 1, wux, 0.0)
+    edge_y = jnp.concatenate(
+        [jnp.where(ylo_mask & has_lo_y, wy[:, :128], 0.0), jnp.where(yhi_mask, wuy[:, last:], 0.0)], axis=1
+    )
+    kterms[10] = edge_y
+    kterms[11] = jnp.where(low_z, jnp.where(last_z, wuz, 0.0), jnp.where(first_z, wz, 0.0))
+
+    rhs = [weight * src[r] for r in range(batch)]
+
+    def exchange(k, fields):
+        for r in range(batch):
+            u_s[k, r] = fields[r]
+            xs[k, 0, r : r + 1, :] = fields[r][0:1]
+            xs[k, 1, r : r + 1, :] = fields[r][side - 1 : side]
+        packed = None
+        for r in range(batch):
+            moved = pltpu.roll(fields[r], jnp.where(low_z, lanes - (side - 1 - r), side - 1 - r), 1)
+            at = jnp.where(low_z, r, side - 1 - r)
+            packed = moved if packed is None else jnp.where(z == at, moved, packed)
+        zs[k] = packed
+        x_lo = copy(xs.at[k, 0], xr.at[k, 1], hsend.at[k, 0], hrecv.at[k, 0], at_x(gx - 1))
+        x_hi = copy(xs.at[k, 1], xr.at[k, 0], hsend.at[k, 1], hrecv.at[k, 1], at_x(gx + 1))
+        y_lo = copy(u_s.at[k, :, :, 0:128], yr.at[k, 1], hsend.at[k, 2], hrecv.at[k, 2], at_y(gy - 1))
+        y_hi = copy(u_s.at[k, :, :, last:lanes], yr.at[k, 0], hsend.at[k, 3], hrecv.at[k, 3], at_y(gy + 1))
+        z_to = copy(zs.at[k], zr.at[k], hsend.at[k, 4], hrecv.at[k, 4], partner)
+        sent = [(x_lo, has_lo_x), (x_hi, has_hi_x), (y_lo, has_lo_y), (y_hi, has_hi_y), (z_to, None)]
+        for c, when in sent:
+            start(c, when)
+        pending.extend(sent)
+        return [(x_lo, has_hi_x), (x_hi, has_lo_x), (y_lo, has_hi_y), (y_hi, has_lo_y), (z_to, None)]
+
+    def moved_by(k, fields, between=None):
+        incoming = exchange(k, fields)
+        terms = [kterms[i] for i in range(6)]
+        acc = [rhs[r] + stencil(fields[r], terms, side) for r in range(batch)]
+        if between is not None:
+            between()
+        for c, when in incoming:
+            wait(c, "recv", when)
+        for r in range(batch):
+            a = kterms[8] * jnp.broadcast_to(xr[k, 0, r : r + 1, :], (side, lanes))
+            a = a + kterms[9] * jnp.broadcast_to(xr[k, 1, r : r + 1, :], (side, lanes))
+            ys = jnp.concatenate([roll(yr[k, 0, r], side, 1), roll(yr[k, 1, r], -side, 1)], axis=1)
+            a = a + kterms[10] * ys
+            zv = pltpu.roll(zr[k], jnp.where(low_z, r, (lanes - r) % lanes), 1) if r else zr[k]
+            a = a + kterms[11] * zv
+            acc[r] = acc[r] + a
+        return acc
+
+    def sweep0(k, fields, between=None):
+        acc = moved_by(k, fields, between)
+        return [(1.0 - OMEGA) * fields[r] + acc[r] for r in range(batch)]
+
+    state = {}
+
+    def coefs_x():
+        landed(g)
+        for i in range(4):
+            cfull[i, mine_x, mine_y] = ctile[i] + czpart[i]
+        state["c"] = gather_x(cfull, cbase)
+
+    def coefs_y():
+        landed(state["c"])
+        state["c"] = gather_y(cfull, cbase)
+
+    nx1, ny1 = gxn * half, gyn * half
+    dims = [(nx1 >> i, ny1 >> i, nz1 >> i) for i in range(LEVELS - 1)]
+    stores = [t1, t2, t3, t4]
+    sels = []
+
+    def coefs_done():
+        landed(state["c"])
+        stack = tuple(cfull[i] for i in range(4))
+        for i, (nx, ny, nz) in enumerate(dims):
+            terms = whole_terms(stack, nx, ny, nz)
+            for j in range(8):
+                stores[i][j] = terms[j]
+            if i + 1 < len(dims):
+                rows, wide = stack[0].shape
+                sel = selector(wide, nz, ny * nz, nz // 2, 0)
+                sels.append(sel)
+                ln = iota2((rows, wide), 1)
+                nxt = coarse_coefs(stack, sel, tmp, (ln // nz) % 2 == 0, (ln % nz) % 2 == 0)
+                if nxt[0].shape[0] < 8:
+                    pad = jnp.zeros((8 - nxt[0].shape[0], 128), F32)
+                    nxt = tuple(jnp.concatenate([a, pad], axis=0) for a in nxt)
+                stack = nxt
+
+    u = list(rhs)
+    u = sweep0(0, u, coefs_x)
+    u = sweep0(1, u, coefs_y)
+    acc = moved_by(2, u, coefs_done)
+    own0 = u
+    res = jnp.concatenate([kterms[7] * (acc[r] - OMEGA * u[r]) for r in range(batch)], axis=0)
+    tmp[0 : batch * side, :] = split_dot(res, sel0)
+    a, b = paired_rows(tmp, batch * half)
+    f1 = a + b
+    for r in range(batch):
+        tile[r] = f1[r * half : (r + 1) * half]
+    landed(gather_z(tile, zpart, 0))
+    for r in range(batch):
+        full[r, mine_x, mine_y] = tile[r] + zpart[r]
+    landed(gather_x(full, 0))
+    landed(gather_y(full, 0))
+
+    def sweeps(fields, wf, i, count):
+        nz = dims[i][2]
+        for _ in range(count):
+            terms = [stores[i][j] for j in range(6)]
+            fields = [
+                (1.0 - OMEGA) * fields[r] + (wf[r] + stencil(fields[r], terms, nz)) for r in range(batch)
+            ]
+        return fields
+
+    f = [full[r] for r in range(batch)]
+    kept = []
+    for i in range(LEVELS - 2):
+        nz = dims[i][2]
+        wf = [stores[i][6] * f[r] for r in range(batch)]
+        v = sweeps(wf, wf, i, NU - 1)
+        kept.append((v, wf))
+        terms = [stores[i][j] for j in range(6)]
+        res = [
+            stores[i][7] * (wf[r] + stencil(v[r], terms, nz) - OMEGA * v[r]) for r in range(batch)
+        ]
+        rows = res[0].shape[0]
+        tmp[0 : batch * rows, :] = split_dot(jnp.concatenate(res, axis=0), sels[i])
+        a, b = paired_rows(tmp, batch * rows // 2)
+        f1 = a + b
+        hr = rows // 2
+        f = [f1[r * hr : (r + 1) * hr] for r in range(batch)]
+        if hr < 8:
+            pad = jnp.zeros((8 - hr, 128), F32)
+            f = [jnp.concatenate([p, pad], axis=0) for p in f]
+    i = LEVELS - 2
+    wf = [stores[i][6] * f[r] for r in range(batch)]
+    v = sweeps(wf, wf, i, KC - 1)
+    for i in range(LEVELS - 3, -1, -1):
+        own, wf = kept[i]
+        rows = own[0].shape[0]
+        wide = doubled_rows(tmp, jnp.concatenate([v[r][: rows // 2] for r in range(batch)], axis=0))
+        up = split_dot(wide, sels[i], transposed=True)
+        v = [own[r] + up[r * rows : (r + 1) * rows] for r in range(batch)]
+        v = sweeps(v, wf, i, NU)
+    for r in range(batch):
+        back[r] = v[r]
+    part = jnp.concatenate([back[r, mine_x, mine_y] for r in range(batch)], axis=0)
+    up = split_dot(doubled_rows(tmp, part), sel0, transposed=True)
+    u = [own0[r] + up[r * side : (r + 1) * side] for r in range(batch)]
+    for s in range(NU):
+        u = sweep0(NU + s, u)
+    for r in range(batch):
+        out[r] = u[r]
+    for c, when in pending:
+        wait(c, "send", when)
+
+
+def kernel_body(peers, source, coef_x, coef_y, coef_z, absorb):
+    gxn, gyn, gzn = peers
+    batch, side, lanes = source.shape
+    half = side // 2
+    nx1 = gxn * half
+    wide = gyn * half * gzn * half
+    ex = 2 * NU
+    row_counts = [max(8, nx1 >> i) for i in range(LEVELS - 1)]
+    scratch = [
+        pltpu.VMEM((ex, batch, side, lanes), F32),
+        pltpu.VMEM((ex, 2, 8, lanes), F32),
+        pltpu.VMEM((ex, 2, 8, lanes), F32),
+        pltpu.VMEM((ex, 2, batch, side, 128), F32),
+        pltpu.VMEM((ex, side, lanes), F32),
+        pltpu.VMEM((ex, side, lanes), F32),
+        pltpu.VMEM((8, lanes), F32),
+        pltpu.VMEM((side, 128), F32),
+        pltpu.VMEM((side, lanes), F32),
+        pltpu.VMEM((4 * nx1 + 64, 128), F32),
+        pltpu.VMEM((batch, half, 128), F32),
+        pltpu.VMEM((batch, half, 128), F32),
+        pltpu.VMEM((batch, nx1, wide), F32),
+        pltpu.VMEM((12, side, lanes), F32),
+        pltpu.VMEM((8, row_counts[0], wide), F32),
+        pltpu.VMEM((8, row_counts[1], 128), F32),
+        pltpu.VMEM((8, row_counts[2], 128), F32),
+        pltpu.VMEM((8, row_counts[3], 128), F32),
+        pltpu.VMEM((4, half, 128), F32),
+        pltpu.VMEM((4, half, 128), F32),
+        pltpu.VMEM((4, nx1, wide), F32),
+        pltpu.VMEM((batch, nx1, wide), F32),
+        pltpu.SemaphoreType.DMA((ex + 1, 5)),
+        pltpu.SemaphoreType.DMA((ex + 1, 5)),
+        pltpu.SemaphoreType.DMA((2 * (gxn + gyn),)),
+        pltpu.SemaphoreType.DMA((2 * (gxn + gyn),)),
+    ]
+    return pl.pallas_call(
+        functools.partial(cycle_kernel, peers, side, batch),
+        out_shape=jax.ShapeDtypeStruct(source.shape, F32),
+        in_specs=[pl.BlockSpec(memory_space=pltpu.VMEM)] * 5,
+        out_specs=pl.BlockSpec(memory_space=pltpu.VMEM),
+        scratch_shapes=scratch,
+        compiler_params=pltpu.CompilerParams(
+            collective_id=0, has_side_effects=True, vmem_limit_bytes=48 * 1024 * 1024
+        ),
+    )(source, coef_x, coef_y, coef_z, absorb)
+
+
 def solution(mesh):
     placed = (
         P(None, "gx", ("gy", "gz")),
@@ -140,6 +584,17 @@
         P("gx", ("gy", "gz")),
         P("gx", ("gy", "gz")),
     )
+    peers = tuple(mesh.shape[a] for a in MESH_AXES)
+
+    def local(source, coef_x, coef_y, coef_z, absorb):
+        side = source.shape[1]
+        half = side // 2
+        fits = peers[0] * peers[1] * peers[2] * half**3 <= GATHER_CELLS
+        fits = fits and peers[2] == 2 and half * half * peers[2] == 128
+        if fits:
+            return kernel_body(peers, source, coef_x, coef_y, coef_z, absorb)
+        return body(source, coef_x, coef_y, coef_z, absorb)
+
     return jax.shard_map(
-        body, mesh=mesh, in_specs=placed, out_specs=P(None, "gx", ("gy", "gz")), check_vma=False
+        local, mesh=mesh, in_specs=placed, out_specs=P(None, "gx", ("gy", "gz")), check_vma=False
     )

time: 828 us -> 45.8 us (0.06); the launches traced: 813 us -> 45.3 us
  waiting for transfers between devices: 378 us -> 0 us
  starting transfers between devices: 336 us -> 0 us
  other arithmetic: 53.5 us -> 0 us
  Pallas kernels: 0 us -> 41 us
  local copies, waits for them, and re-layouts: 38.3 us -> 4.29 us
  between operations: 8.38 us -> 0.01 us
    ppermute x201 -> x0, waiting for transfers between devices: 378 us -> none  [the longest x93 351 us: extended(): after = lax.ppermute(first, axis, down)]
    ppermute x201 -> x0, starting transfers between devices: 336 us -> none  [the longest x93 195 us: extended(): before = lax.ppermute(last, axis, up)]
    add x35 -> x0, other arithmetic: 43.5 us -> none  [the longest x27 42.4 us: smooth(): field + OMEGA * (rhs - apply_padded(padded_shard(field), terms)) / terms[7]]
    pallas_call x0 -> x1, Pallas kernels: none -> 41 us  [kernel_body(): pl.pallas_call(functools.partial(cycle_kernel, peers, side, batch), out_s...]
    slice x85 -> x0, local copies, waits for them, and re-layouts: 13 us -> none  [the longest x60 7.5 us: extended(): last = lax.slice_in_dim(array, length - width, length, axis=dim)]
    reshape x25 -> x0, local copies, waits for them, and re-layouts: 11.4 us -> none  [the longest x6 2.87 us: coarsen_coef(): blocks = coef.reshape(sizes[0] // 2, 2, sizes[1] // 2, 2, sizes[2] // 2, 2)]
  transfers between devices with their start and end apart: 201 -> 0, of which waited for: 112 -> 0; matrix products, arithmetic and copies ran while one was open for 4% -> 0% of each run, Pallas kernels for 0% -> 0%
where the time goes in v1:
time: 45.8 us; the launch traced here: 45.3 us
  Pallas kernels  41 us (90%)
  local copies, waits for them, and re-layouts  4.29 us (9%)
    pallas_call x1, Pallas kernels, kernel_body(): pl.pallas_call(functools.partial(cycle_kernel, peers, side, batch), out_s...  41 us
    unnamed x11, local copies, waits for them, and re-layouts  4.29 us

profile of v1, /device:TPU:0, one launch (start us, length us, event | category | flops | bytes accessed | tf_op | source)
XLA Modules:
  0.0 45.3 jit_solution(9379297258256608868)
XLA Ops:
  0.0 0.0 copy-start
  0.0 0.8 %copy-done = f32[3,16,256]{2,1,0:T(8,128)S(1)} copy-done((f32[3,16,256]{2,1,0:T(8,128)S(1)}, f32[3,16,256]{2,1,0:T(8,128)}, u32[]{:S(2)}) %copy-start) | copy-done | bytes 49176
  0.8 0.0 copy-start.1
  0.8 0.7 %copy-done.1 = f32[16,256]{1,0:T(8,128)S(1)} copy-done((f32[16,256]{1,0:T(8,128)S(1)}, f32[16,256]{1,0:T(8,128)}, u32[]{:S(2)}) %copy-start.1) | copy-done | bytes 16408
  1.5 0.0 copy-start.2
  1.5 0.7 %copy-done.2 = f32[16,256]{1,0:T(8,128)S(1)} copy-done((f32[16,256]{1,0:T(8,128)S(1)}, f32[16,256]{1,0:T(8,128)}, u32[]{:S(2)}) %copy-start.2) | copy-done | bytes 16408
  2.2 0.0 copy-start.3
  2.2 0.7 %copy-done.3 = f32[16,256]{1,0:T(8,128)S(1)} copy-done((f32[16,256]{1,0:T(8,128)S(1)}, f32[16,256]{1,0:T(8,128)}, u32[]{:S(2)}) %copy-start.3) | copy-done | bytes 16408
  3.0 0.0 copy-start.4
  3.0 0.7 %copy-done.4 = f32[16,256]{1,0:T(8,128)S(1)} copy-done((f32[16,256]{1,0:T(8,128)S(1)}, f32[16,256]{1,0:T(8,128)}, u32[]{:S(2)}) %copy-start.4) | copy-done | bytes 16408
  3.7 41.0 %shard_map.55 = f32[3,16,256]{2,1,0:T(8,128)S(1)} custom-call(f32[3,16,256]{2,1,0:T(8,128)S(1)} %copy-done, f32[16,256]{1,0:T(8,128)S(1)} %copy-done.1, f32[16,256]{1,0:T(8,128)S(1)} %copy-done.2, f32[16,256]{1,0:T(8,128)S(1)} %copy-done.3, f32[16,256]{1,0:T(8,128)S(1)} %copy-done.4), custom_call_target="tpu_custom_call" | custom-call | tf_op jit(solution)/shard_map/pallas_call | solution.py:567
  44.7 0.6 %copy.7 = f32[3,16,256]{2,1,0:T(8,128)} copy(f32[3,16,256]{2,1,0:T(8,128)S(1)} %shard_map.55) | data formatting | bytes 98304
Async XLA Ops:
  0.0 0.8 %copy-start = (f32[3,16,256]{2,1,0:T(8,128)S(1)}, f32[3,16,256]{2,1,0:T(8,128)}, u32[]{:S(2)}) copy-start(f32[3,16,256]{2,1,0:T(8,128)} %src.1) | copy-start | bytes 147460
  0.8 0.7 %copy-start.1 = (f32[16,256]{1,0:T(8,128)S(1)}, f32[16,256]{1,0:T(8,128)}, u32[]{:S(2)}) copy-start(f32[16,256]{1,0:T(8,128)} %kx_ref.1) | copy-start | bytes 49156
  1.5 0.7 %copy-start.2 = (f32[16,256]{1,0:T(8,128)S(1)}, f32[16,256]{1,0:T(8,128)}, u32[]{:S(2)}) copy-start(f32[16,256]{1,0:T(8,128)} %ky_ref.1) | copy-start | bytes 49156
  2.2 0.7 %copy-start.3 = (f32[16,256]{1,0:T(8,128)S(1)}, f32[16,256]{1,0:T(8,128)}, u32[]{:S(2)}) copy-start(f32[16,256]{1,0:T(8,128)} %kz_ref.1) | copy-start | bytes 49156
  3.0 0.7 %copy-start.4 = (f32[16,256]{1,0:T(8,128)S(1)}, f32[16,256]{1,0:T(8,128)}, u32[]{:S(2)}) copy-start(f32[16,256]{1,0:T(8,128)} %sa_ref.1) | copy-start | bytes 49156

commit v2 on v1

--- a/solution.py
+++ b/solution.py
@@ -150,13 +150,12 @@
     dims = (((1,), (1,)), ((), ())) if transposed else (((1,), (0,)), ((), ()))
     high = values.astype(BF16)
     rest = values - high.astype(F32)
-    mid = rest.astype(BF16)
-    low = (rest - mid.astype(F32)).astype(BF16)
+    low = rest.astype(BF16)
 
     def one(part):
         return lax.dot_general(part, selector, dims, preferred_element_type=F32)
 
-    return one(high) + (one(mid) + one(low))
+    return one(high) + one(low)
 
 
 def selector(lanes, nz, cells, coarse_nz, offset):
@@ -227,9 +226,9 @@
     )
 
 
-def cycle_kernel(peers, side, batch, src, kx_ref, ky_ref, kz_ref, sa_ref, out, u_s, xs, xr, yr, zs, zr,
-                 cxr, cyr, czr, tmp, tile, zpart, full, kterms, t1, t2, t3, t4, ctile, czpart, cfull, back,
-                 hsend, hrecv, gsend, grecv):
+def cycle_kernel(peers, side, batch, src_h, kx_h, ky_h, kz_h, sa_h, out, src, kx_ref, ky_ref, kz_ref, sa_ref, u_s, xs, xr, yr, zs, zr,
+                 cxr, cyr, czr, tmp, full, kterms, t1, t2, t3, t4, cfull, back,
+                 col, zcol, ccol, czcol, hsend, hrecv, gsend, grecv, lsem):
     gxn, gyn, gzn = peers
     gx, gy, gz = lax.axis_index("gx"), lax.axis_index("gy"), lax.axis_index("gz")
     lanes = side * side
@@ -245,8 +244,12 @@
     partner = (gx, gy, 1 - gz)
     others = [at_x(lax.rem(gx + d, gxn)) for d in range(1, gxn)]
     others += [at_y(lax.rem(gy + d, gyn)) for d in range(1, gyn)]
-    others += [partner]
-
+    others += [(lax.rem(gx + d, gxn), gy, 1 - gz) for d in range(gxn)]
+
+    loads = []
+    for i, (a, b) in enumerate(((kx_h, kx_ref), (ky_h, ky_ref), (kz_h, kz_ref), (sa_h, sa_ref), (src_h, src))):
+        loads.append(pltpu.make_async_copy(a, b, lsem.at[i]))
+        loads[i].start()
     xs[...] = jnp.zeros_like(xs)
     xr[...] = jnp.zeros_like(xr)
     yr[...] = jnp.zeros_like(yr)
@@ -256,6 +259,8 @@
     barrier = pltpu.get_barrier_semaphore()
     for peer in others:
         pl.semaphore_signal(barrier, inc=1, device_id=peer, device_id_type=MESH)
+    for c in loads:
+        c.wait()
     pl.semaphore_wait(barrier, len(others))
 
     pending = []
@@ -281,7 +286,7 @@
     has_lo_x, has_hi_x = gx > 0, gx < gxn - 1
     has_lo_y, has_hi_y = gy > 0, gy < gyn - 1
 
-    nk = NU * 2
+    nk = NU * 2 - 1
     c_x = copy(kx_ref.at[0:8], cxr, hsend.at[nk, 0], hrecv.at[nk, 0], at_x(gx - 1))
     c_y = copy(ky_ref.at[:, 0:128], cyr, hsend.at[nk, 1], hrecv.at[nk, 1], at_y(gy - 1))
     c_z = copy(kz_ref, czr, hsend.at[nk, 2], hrecv.at[nk, 2], partner)
@@ -297,24 +302,36 @@
     half = side // 2
     nz1 = half * gzn
     sel0 = selector(lanes, side, lanes, nz1, gz * half)
+    fine = iota2((lanes, 128), 0)
+    fine_y, fine_z = fine // side, fine % side
+    coarse_at = iota2((lanes, 128), 1)
+
+    def picked(hit):
+        return jnp.where(hit, 1.0, 0.0).astype(BF16)
+
+    sel_z = picked(
+        (fine_z == jnp.where(gz == 0, side - 1, 0))
+        & (coarse_at == fine_y // 2 * nz1 + jnp.where(gz == 0, half, half - 1))
+    )
+    in_row = gz * half + fine_z // 2
+    sel_ylo = picked((fine_y == 0) & (coarse_at == (half - 1) * nz1 + in_row))
+    sel_yhi = picked((fine_y == side - 1) & (coarse_at == in_row))
     even_y, even_z = (y % 2) == 0, (z % 2) == 0
     coarse = coarse_coefs((kx, ky, kz, sa), sel0, tmp, even_y, even_z)
+    mine_x, mine_y = pl.ds(pl.multiple_of(gx * half, half), half), pl.ds(pl.multiple_of(gy * 128, 128), 128)
     for i in range(4):
-        ctile[i] = coarse[i]
-
-    mine_x, mine_y = pl.ds(pl.multiple_of(gx * half, half), half), pl.ds(pl.multiple_of(gy * 128, 128), 128)
-
-    def gather_z(a, b, base):
-        c = copy(a, b, gsend.at[base], grecv.at[base], partner)
-        start(c)
-        pending.append((c, None))
-        return [c]
-
-    def gather_x(whole, base):
+        ccol[i, mine_x] = coarse[i]
+
+    def gather_xz(mine, other, base):
         cs = []
-        for d in range(1, gxn):
-            ref = whole.at[:, mine_x, mine_y]
-            cs.append(copy(ref, ref, gsend.at[base + d], grecv.at[base + d], at_x(lax.rem(gx + d, gxn))))
+        for d in range(gxn):
+            at = lax.rem(gx + d, gxn)
+            ref = mine.at[:, mine_x]
+            if d > 0:
+                cs.append(copy(ref, ref, gsend.at[base + d], grecv.at[base + d], at_x(at)))
+            cs.append(
+                copy(ref, other.at[:, mine_x], gsend.at[base + gxn + d], grecv.at[base + gxn + d], (at, gy, 1 - gz))
+            )
         for c in cs:
             start(c)
             pending.append((c, None))
@@ -325,7 +342,7 @@
         for d in range(1, gyn):
             ref = whole.at[:, :, mine_y]
             cs.append(
-                copy(ref, ref, gsend.at[base + gxn + d], grecv.at[base + gxn + d], at_y(lax.rem(gy + d, gyn)))
+                copy(ref, ref, gsend.at[base + 2 * gxn + d], grecv.at[base + 2 * gxn + d], at_y(lax.rem(gy + d, gyn)))
             )
         for c in cs:
             start(c)
@@ -336,8 +353,8 @@
         for c in cs:
             wait(c, "recv")
 
-    cbase = gxn + gyn
-    g = gather_z(ctile, czpart, cbase)
+    cbase = 2 * gxn + gyn
+    g = gather_xz(ccol, czcol, cbase)
 
     wait(c_x, "recv", has_hi_x)
     wait(c_y, "recv", has_hi_y)
@@ -410,6 +427,7 @@
             between()
         for c, when in incoming:
             wait(c, "recv", when)
+        state["faces"] = []
         for r in range(batch):
             a = kterms[8] * jnp.broadcast_to(xr[k, 0, r : r + 1, :], (side, lanes))
             a = a + kterms[9] * jnp.broadcast_to(xr[k, 1, r : r + 1, :], (side, lanes))
@@ -417,6 +435,7 @@
             a = a + kterms[10] * ys
             zv = pltpu.roll(zr[k], jnp.where(low_z, r, (lanes - r) % lanes), 1) if r else zr[k]
             a = a + kterms[11] * zv
+            state["faces"].append(a)
             acc[r] = acc[r] + a
         return acc
 
@@ -426,14 +445,10 @@
 
     state = {}
 
-    def coefs_x():
+    def coefs_y():
         landed(g)
         for i in range(4):
-            cfull[i, mine_x, mine_y] = ctile[i] + czpart[i]
-        state["c"] = gather_x(cfull, cbase)
-
-    def coefs_y():
-        landed(state["c"])
+            cfull[i, :, mine_y] = ccol[i] + czcol[i]
         state["c"] = gather_y(cfull, cbase)
 
     nx1, ny1 = gxn * half, gyn * half
@@ -460,20 +475,20 @@
                 stack = nxt
 
     u = list(rhs)
-    u = sweep0(0, u, coefs_x)
+    u = sweep0(0, u)
     u = sweep0(1, u, coefs_y)
     acc = moved_by(2, u, coefs_done)
     own0 = u
+    faces = state["faces"]
     res = jnp.concatenate([kterms[7] * (acc[r] - OMEGA * u[r]) for r in range(batch)], axis=0)
     tmp[0 : batch * side, :] = split_dot(res, sel0)
     a, b = paired_rows(tmp, batch * half)
     f1 = a + b
     for r in range(batch):
-        tile[r] = f1[r * half : (r + 1) * half]
-    landed(gather_z(tile, zpart, 0))
+        col[r, mine_x] = f1[r * half : (r + 1) * half]
+    landed(gather_xz(col, zcol, 0))
     for r in range(batch):
-        full[r, mine_x, mine_y] = tile[r] + zpart[r]
-    landed(gather_x(full, 0))
+        full[r, :, mine_y] = col[r] + zcol[r]
     landed(gather_y(full, 0))
 
     def sweeps(fields, wf, i, count):
@@ -517,11 +532,39 @@
         v = sweeps(v, wf, i, NU)
     for r in range(batch):
         back[r] = v[r]
-    part = jnp.concatenate([back[r, mine_x, mine_y] for r in range(batch)], axis=0)
-    up = split_dot(doubled_rows(tmp, part), sel0, transposed=True)
-    u = [own0[r] + up[r * side : (r + 1) * side] for r in range(batch)]
-    for s in range(NU):
-        u = sweep0(NU + s, u)
+
+    def tiles(at_rows, at_lanes):
+        return jnp.concatenate([back[r, at_rows, at_lanes] for r in range(batch)], axis=0)
+
+    def rows_at(i):
+        return pl.ds(pl.multiple_of(i * half, half), half)
+
+    def lanes_at(i):
+        return pl.ds(pl.multiple_of(i * 128, 128), 128)
+
+    below_y, above_y = jnp.maximum(gy - 1, 0), jnp.minimum(gy + 1, gyn - 1)
+    part = doubled_rows(tmp, tiles(mine_x, mine_y))
+    up = split_dot(part, sel0, transposed=True)
+    beside_z = split_dot(part, sel_z, transposed=True)
+    edge_lo = doubled_rows(tmp, tiles(mine_x, lanes_at(below_y)))
+    edge_hi = doubled_rows(tmp, tiles(mine_x, lanes_at(above_y)))
+    beside_y = split_dot(edge_lo, sel_ylo, transposed=True) + split_dot(edge_hi, sel_yhi, transposed=True)
+    edge_x = jnp.concatenate(
+        [tiles(rows_at(jnp.maximum(gx - 1, 0)), mine_y), tiles(rows_at(jnp.minimum(gx + 1, gxn - 1)), mine_y)], axis=0
+    )
+    beside_x = split_dot(edge_x, sel0, transposed=True)
+    u = []
+    terms = [kterms[i] for i in range(6)]
+    for r in range(batch):
+        v0 = own0[r] + up[r * side : (r + 1) * side]
+        lo = beside_x[(r + 1) * half - 1 : (r + 1) * half]
+        hi = beside_x[(batch + r) * half : (batch + r) * half + 1]
+        a = kterms[8] * jnp.broadcast_to(lo, (side, lanes)) + kterms[9] * jnp.broadcast_to(hi, (side, lanes))
+        a = a + kterms[10] * beside_y[r * side : (r + 1) * side]
+        a = a + kterms[11] * beside_z[r * side : (r + 1) * side]
+        u.append((1.0 - OMEGA) * v0 + (rhs[r] + stencil(v0, terms, side) + faces[r] + a))
+    for s in range(1, NU):
+        u = sweep0(NU + s - 1, u)
     for r in range(batch):
         out[r] = u[r]
     for c, when in pending:
@@ -534,9 +577,14 @@
     half = side // 2
     nx1 = gxn * half
     wide = gyn * half * gzn * half
-    ex = 2 * NU
+    ex = 2 * NU - 1
     row_counts = [max(8, nx1 >> i) for i in range(LEVELS - 1)]
     scratch = [
+        pltpu.VMEM((batch, side, lanes), F32),
+        pltpu.VMEM((side, lanes), F32),
+        pltpu.VMEM((side, lanes), F32),
+        pltpu.VMEM((side, lanes), F32),
+        pltpu.VMEM((side, lanes), F32),
         pltpu.VMEM((ex, batch, side, lanes), F32),
         pltpu.VMEM((ex, 2, 8, lanes), F32),
         pltpu.VMEM((ex, 2, 8, lanes), F32),
@@ -547,27 +595,28 @@
         pltpu.VMEM((side, 128), F32),
         pltpu.VMEM((side, lanes), F32),
         pltpu.VMEM((4 * nx1 + 64, 128), F32),
-        pltpu.VMEM((batch, half, 128), F32),
-        pltpu.VMEM((batch, half, 128), F32),
         pltpu.VMEM((batch, nx1, wide), F32),
         pltpu.VMEM((12, side, lanes), F32),
         pltpu.VMEM((8, row_counts[0], wide), F32),
         pltpu.VMEM((8, row_counts[1], 128), F32),
         pltpu.VMEM((8, row_counts[2], 128), F32),
         pltpu.VMEM((8, row_counts[3], 128), F32),
-        pltpu.VMEM((4, half, 128), F32),
-        pltpu.VMEM((4, half, 128), F32),
         pltpu.VMEM((4, nx1, wide), F32),
         pltpu.VMEM((batch, nx1, wide), F32),
+        pltpu.VMEM((batch, nx1, 128), F32),
+        pltpu.VMEM((batch, nx1, 128), F32),
+        pltpu.VMEM((4, nx1, 128), F32),
+        pltpu.VMEM((4, nx1, 128), F32),
         pltpu.SemaphoreType.DMA((ex + 1, 5)),
         pltpu.SemaphoreType.DMA((ex + 1, 5)),
-        pltpu.SemaphoreType.DMA((2 * (gxn + gyn),)),
-        pltpu.SemaphoreType.DMA((2 * (gxn + gyn),)),
+        pltpu.SemaphoreType.DMA((2 * (2 * gxn + gyn),)),
+        pltpu.SemaphoreType.DMA((2 * (2 * gxn + gyn),)),
+        pltpu.SemaphoreType.DMA((5,)),
     ]
     return pl.pallas_call(
         functools.partial(cycle_kernel, peers, side, batch),
         out_shape=jax.ShapeDtypeStruct(source.shape, F32),
-        in_specs=[pl.BlockSpec(memory_space=pltpu.VMEM)] * 5,
+        in_specs=[pl.BlockSpec(memory_space=pl.ANY)] * 5,
         out_specs=pl.BlockSpec(memory_space=pltpu.VMEM),
         scratch_shapes=scratch,
         compiler_params=pltpu.CompilerParams(

time: 45.8 us -> 41.3 us (0.902)
  Pallas kernels: 41 us -> 36.5 us
    pallas_call x1, Pallas kernels: 41 us -> 36.5 us  [kernel_body(): pl.pallas_call(functools.partial(cycle_kernel, peers, side, batch), out_s...]
where the time goes in v2:
time: 41.3 us; the launch traced here: 40.8 us
  Pallas kernels  36.5 us (88%)
  local copies, waits for them, and re-layouts  4.29 us (10%)
    pallas_call x1, Pallas kernels, kernel_body(): pl.pallas_call(functools.partial(cycle_kernel, peers, side, batch), out_s...  36.5 us
    unnamed x11, local copies, waits for them, and re-layouts  4.29 us

profile of v2, /device:TPU:0, one launch (start us, length us, event | category | flops | bytes accessed | tf_op | source)
XLA Modules:
  0.0 40.8 jit_solution(14658373210823324662)
XLA Ops:
  0.0 0.0 copy-start
  0.0 0.8 %copy-done = f32[3,16,256]{2,1,0:T(8,128)S(1)} copy-done((f32[3,16,256]{2,1,0:T(8,128)S(1)}, f32[3,16,256]{2,1,0:T(8,128)}, u32[]{:S(2)}) %copy-start) | copy-done | bytes 49176
  0.8 0.0 copy-start.1
  0.8 0.7 %copy-done.1 = f32[16,256]{1,0:T(8,128)S(1)} copy-done((f32[16,256]{1,0:T(8,128)S(1)}, f32[16,256]{1,0:T(8,128)}, u32[]{:S(2)}) %copy-start.1) | copy-done | bytes 16408
  1.5 0.0 copy-start.2
  1.5 0.7 %copy-done.2 = f32[16,256]{1,0:T(8,128)S(1)} copy-done((f32[16,256]{1,0:T(8,128)S(1)}, f32[16,256]{1,0:T(8,128)}, u32[]{:S(2)}) %copy-start.2) | copy-done | bytes 16408
  2.2 0.0 copy-start.3
  2.2 0.7 %copy-done.3 = f32[16,256]{1,0:T(8,128)S(1)} copy-done((f32[16,256]{1,0:T(8,128)S(1)}, f32[16,256]{1,0:T(8,128)}, u32[]{:S(2)}) %copy-start.3) | copy-done | bytes 16408
  3.0 0.0 copy-start.4
  3.0 0.7 %copy-done.4 = f32[16,256]{1,0:T(8,128)S(1)} copy-done((f32[16,256]{1,0:T(8,128)S(1)}, f32[16,256]{1,0:T(8,128)}, u32[]{:S(2)}) %copy-start.4) | copy-done | bytes 16408
  3.7 36.5 %shard_map.55 = f32[3,16,256]{2,1,0:T(8,128)S(1)} custom-call(f32[3,16,256]{2,1,0:T(8,128)S(1)} %copy-done, f32[16,256]{1,0:T(8,128)S(1)} %copy-done.1, f32[16,256]{1,0:T(8,128)S(1)} %copy-done.2, f32[16,256]{1,0:T(8,128)S(1)} %copy-done.3, f32[16,256]{1,0:T(8,128)S(1)} %copy-done.4), custom_call_target="tpu_custom_call" | custom-call | tf_op jit(solution)/shard_map/pallas_call | solution.py:616
  40.2 0.6 %copy.7 = f32[3,16,256]{2,1,0:T(8,128)} copy(f32[3,16,256]{2,1,0:T(8,128)S(1)} %shard_map.55) | data formatting | bytes 98304
Async XLA Ops:
  0.0 0.8 %copy-start = (f32[3,16,256]{2,1,0:T(8,128)S(1)}, f32[3,16,256]{2,1,0:T(8,128)}, u32[]{:S(2)}) copy-start(f32[3,16,256]{2,1,0:T(8,128)} %src_h.1) | copy-start | bytes 147460
  0.8 0.7 %copy-start.1 = (f32[16,256]{1,0:T(8,128)S(1)}, f32[16,256]{1,0:T(8,128)}, u32[]{:S(2)}) copy-start(f32[16,256]{1,0:T(8,128)} %kx_h.1) | copy-start | bytes 49156
  1.5 0.7 %copy-start.2 = (f32[16,256]{1,0:T(8,128)S(1)}, f32[16,256]{1,0:T(8,128)}, u32[]{:S(2)}) copy-start(f32[16,256]{1,0:T(8,128)} %ky_h.1) | copy-start | bytes 49156
  2.2 0.7 %copy-start.3 = (f32[16,256]{1,0:T(8,128)S(1)}, f32[16,256]{1,0:T(8,128)}, u32[]{:S(2)}) copy-start(f32[16,256]{1,0:T(8,128)} %kz_h.1) | copy-start | bytes 49156
  3.0 0.7 %copy-start.4 = (f32[16,256]{1,0:T(8,128)S(1)}, f32[16,256]{1,0:T(8,128)}, u32[]{:S(2)}) copy-start(f32[16,256]{1,0:T(8,128)} %sa_h.1) | copy-start | bytes 49156

commit v3 on v2

--- a/solution.py
+++ b/solution.py
@@ -259,6 +259,29 @@
     barrier = pltpu.get_barrier_semaphore()
     for peer in others:
         pl.semaphore_signal(barrier, inc=1, device_id=peer, device_id_type=MESH)
+    half = side // 2
+    nz1 = half * gzn
+    sel0 = selector(lanes, side, lanes, nz1, gz * half)
+    fine = iota2((lanes, 128), 0)
+    fine_y, fine_z = fine // side, fine % side
+    coarse_at = iota2((lanes, 128), 1)
+
+    def picked(hit):
+        return jnp.where(hit, 1.0, 0.0).astype(BF16)
+
+    sel_z = picked(
+        (fine_z == jnp.where(gz == 0, side - 1, 0))
+        & (coarse_at == fine_y // 2 * nz1 + jnp.where(gz == 0, half, half - 1))
+    )
+    in_row = gz * half + fine_z // 2
+    sel_ylo = picked((fine_y == 0) & (coarse_at == (half - 1) * nz1 + in_row))
+    sel_yhi = picked((fine_y == side - 1) & (coarse_at == in_row))
+    nx1, ny1 = gxn * half, gyn * half
+    dims = [(nx1 >> i, ny1 >> i, nz1 >> i) for i in range(LEVELS - 1)]
+    widths = [ny1 * nz1] + [128] * (LEVELS - 3)
+    sels = [
+        selector(widths[i], dims[i][2], dims[i][1] * dims[i][2], dims[i][2] // 2, 0) for i in range(LEVELS - 2)
+    ]
     for c in loads:
         c.wait()
     pl.semaphore_wait(barrier, len(others))
@@ -299,23 +322,6 @@
     x = iota2((side, lanes), 0)
     lane = iota2((side, lanes), 1)
     y, z = lane // side, lane % side
-    half = side // 2
-    nz1 = half * gzn
-    sel0 = selector(lanes, side, lanes, nz1, gz * half)
-    fine = iota2((lanes, 128), 0)
-    fine_y, fine_z = fine // side, fine % side
-    coarse_at = iota2((lanes, 128), 1)
-
-    def picked(hit):
-        return jnp.where(hit, 1.0, 0.0).astype(BF16)
-
-    sel_z = picked(
-        (fine_z == jnp.where(gz == 0, side - 1, 0))
-        & (coarse_at == fine_y // 2 * nz1 + jnp.where(gz == 0, half, half - 1))
-    )
-    in_row = gz * half + fine_z // 2
-    sel_ylo = picked((fine_y == 0) & (coarse_at == (half - 1) * nz1 + in_row))
-    sel_yhi = picked((fine_y == side - 1) & (coarse_at == in_row))
     even_y, even_z = (y % 2) == 0, (z % 2) == 0
     coarse = coarse_coefs((kx, ky, kz, sa), sel0, tmp, even_y, even_z)
     mine_x, mine_y = pl.ds(pl.multiple_of(gx * half, half), half), pl.ds(pl.multiple_of(gy * 128, 128), 128)
@@ -451,10 +457,7 @@
             cfull[i, :, mine_y] = ccol[i] + czcol[i]
         state["c"] = gather_y(cfull, cbase)
 
-    nx1, ny1 = gxn * half, gyn * half
-    dims = [(nx1 >> i, ny1 >> i, nz1 >> i) for i in range(LEVELS - 1)]
     stores = [t1, t2, t3, t4]
-    sels = []
 
     def coefs_done():
         landed(state["c"])
@@ -465,8 +468,7 @@
                 stores[i][j] = terms[j]
             if i + 1 < len(dims):
                 rows, wide = stack[0].shape
-                sel = selector(wide, nz, ny * nz, nz // 2, 0)
-                sels.append(sel)
+                sel = sels[i]
                 ln = iota2((rows, wide), 1)
                 nxt = coarse_coefs(stack, sel, tmp, (ln // nz) % 2 == 0, (ln % nz) % 2 == 0)
                 if nxt[0].shape[0] < 8:
@@ -616,7 +618,7 @@
     return pl.pallas_call(
         functools.partial(cycle_kernel, peers, side, batch),
         out_shape=jax.ShapeDtypeStruct(source.shape, F32),
-        in_specs=[pl.BlockSpec(memory_space=pl.ANY)] * 5,
+        in_specs=[pl.BlockSpec(memory_space=pltpu.HBM)] * 5,
         out_specs=pl.BlockSpec(memory_space=pltpu.VMEM),
         scratch_shapes=scratch,
         compiler_params=pltpu.CompilerParams(

time: 41.3 us -> 41.2 us (level)
  no operation moved by 1% of the time
where the time goes in v3:
time: 41.2 us; the launch traced here: 40.7 us
  Pallas kernels  36.4 us (88%)
  local copies, waits for them, and re-layouts  4.29 us (10%)
    pallas_call x1, Pallas kernels, kernel_body(): pl.pallas_call(functools.partial(cycle_kernel, peers, side, batch), out_s...  36.4 us
    unnamed x11, local copies, waits for them, and re-layouts  4.29 us

profile of v3, /device:TPU:0, one launch (start us, length us, event | category | flops | bytes accessed | tf_op | source)
XLA Modules:
  0.0 40.7 jit_solution(18324837912661082769)
XLA Ops:
  0.0 0.0 copy-start
  0.0 0.8 %copy-done = f32[3,16,256]{2,1,0:T(8,128)S(1)} copy-done((f32[3,16,256]{2,1,0:T(8,128)S(1)}, f32[3,16,256]{2,1,0:T(8,128)}, u32[]{:S(2)}) %copy-start) | copy-done | bytes 49176
  0.8 0.0 copy-start.1
  0.8 0.7 %copy-done.1 = f32[16,256]{1,0:T(8,128)S(1)} copy-done((f32[16,256]{1,0:T(8,128)S(1)}, f32[16,256]{1,0:T(8,128)}, u32[]{:S(2)}) %copy-start.1) | copy-done | bytes 16408
  1.5 0.0 copy-start.2
  1.5 0.7 %copy-done.2 = f32[16,256]{1,0:T(8,128)S(1)} copy-done((f32[16,256]{1,0:T(8,128)S(1)}, f32[16,256]{1,0:T(8,128)}, u32[]{:S(2)}) %copy-start.2) | copy-done | bytes 16408
  2.2 0.0 copy-start.3
  2.2 0.7 %copy-done.3 = f32[16,256]{1,0:T(8,128)S(1)} copy-done((f32[16,256]{1,0:T(8,128)S(1)}, f32[16,256]{1,0:T(8,128)}, u32[]{:S(2)}) %copy-start.3) | copy-done | bytes 16408
  3.0 0.0 copy-start.4
  3.0 0.7 %copy-done.4 = f32[16,256]{1,0:T(8,128)S(1)} copy-done((f32[16,256]{1,0:T(8,128)S(1)}, f32[16,256]{1,0:T(8,128)}, u32[]{:S(2)}) %copy-start.4) | copy-done | bytes 16408
  3.7 36.4 %shard_map.55 = f32[3,16,256]{2,1,0:T(8,128)S(1)} custom-call(f32[3,16,256]{2,1,0:T(8,128)S(1)} %copy-done, f32[16,256]{1,0:T(8,128)S(1)} %copy-done.1, f32[16,256]{1,0:T(8,128)S(1)} %copy-done.2, f32[16,256]{1,0:T(8,128)S(1)} %copy-done.3, f32[16,256]{1,0:T(8,128)S(1)} %copy-done.4), custom_call_target="tpu_custom_call" | custom-call | tf_op jit(solution)/shard_map/pallas_call | solution.py:618
  40.1 0.6 %copy.7 = f32[3,16,256]{2,1,0:T(8,128)} copy(f32[3,16,256]{2,1,0:T(8,128)S(1)} %shard_map.55) | data formatting | bytes 98304
Async XLA Ops:
  0.0 0.8 %copy-start = (f32[3,16,256]{2,1,0:T(8,128)S(1)}, f32[3,16,256]{2,1,0:T(8,128)}, u32[]{:S(2)}) copy-start(f32[3,16,256]{2,1,0:T(8,128)} %src_h.1) | copy-start | bytes 147460
  0.8 0.7 %copy-start.1 = (f32[16,256]{1,0:T(8,128)S(1)}, f32[16,256]{1,0:T(8,128)}, u32[]{:S(2)}) copy-start(f32[16,256]{1,0:T(8,128)} %kx_h.1) | copy-start | bytes 49156
  1.5 0.7 %copy-start.2 = (f32[16,256]{1,0:T(8,128)S(1)}, f32[16,256]{1,0:T(8,128)}, u32[]{:S(2)}) copy-start(f32[16,256]{1,0:T(8,128)} %ky_h.1) | copy-start | bytes 49156
  2.2 0.7 %copy-start.3 = (f32[16,256]{1,0:T(8,128)S(1)}, f32[16,256]{1,0:T(8,128)}, u32[]{:S(2)}) copy-start(f32[16,256]{1,0:T(8,128)} %kz_h.1) | copy-start | bytes 49156
  3.0 0.7 %copy-start.4 = (f32[16,256]{1,0:T(8,128)S(1)}, f32[16,256]{1,0:T(8,128)}, u32[]{:S(2)}) copy-start(f32[16,256]{1,0:T(8,128)} %sa_h.1) | copy-start | bytes 49156
